TPU v7x, 512 devices: a whole 4x8x8 slice. The times are simulated.
512 devices in a mesh: dp: 32 (over x, z), hid: 16 (over y, core).
Axes of the slice: x: 4, y: 8, z: 8, core: 2. Of those that a mesh axis runs over, the one named last changes fastest.
Arguments:
- inputs: bfloat16 [8192, 8192], P('dp', 'hid'), may hold values from -6 to 6
- out_grad: bfloat16 [8192, 8192], P('dp', 'hid'), may hold values from -6 to 6
- home_block: int32 [64], P('hid'), may hold values from 0 to 1
- blocks_up: bfloat16 [64, 3, 256, 256], P('hid', None, 'dp'), may hold values from -0.21875 to 0.21875
- blocks_down: bfloat16 [64, 3, 256, 256], P('hid', None, 'dp'), may hold values from -0.15625 to 0.15625
- up_left: bfloat16 [8192, 128], P('hid', 'dp'), may hold values from -0.0625 to 0.0625
- up_right: bfloat16 [128, 16384], P('dp', 'hid'), may hold values from -0.5 to 0.5
- down_left: bfloat16 [16384, 128], P('hid', 'dp'), may hold values from -0.046875 to 0.046875
- down_right: bfloat16 [128, 8192], P('dp', 'hid'), may hold values from -0.5 to 0.5
Outputs:
- outputs: bfloat16 [8192, 8192], P('dp', 'hid')
- input_grad: bfloat16 [8192, 8192], P('dp', 'hid')
- grad_blocks_up: bfloat16 [64, 3, 256, 256], P('hid', None, 'dp')
- grad_blocks_down: bfloat16 [64, 3, 256, 256], P('hid', None, 'dp')
- grad_up_left: bfloat16 [8192, 128], P('hid', 'dp')
- grad_up_right: bfloat16 [128, 16384], P('dp', 'hid')
- grad_down_left: bfloat16 [16384, 128], P('hid', 'dp')
- grad_down_right: bfloat16 [128, 8192], P('dp', 'hid')
All inputs are finite; a program needn't handle non-finite values.
Results may differ from a plain program's by a relative error of at most 0.022.
Values may be sent and summed in bfloat16 or wider, within the bound.
A program may use at most 64 MiB of HBM per device.

v0:
```python
import jax
import jax.numpy as jnp
from jax import lax
from jax.sharding import PartitionSpec as P

gelu_coef = 0.7978845608028654
cubic_coef = 0.044715


def from_partner(value, axis, distance):
    mask = 2**distance
    pairs = [(source, source ^ mask) for source in range(lax.axis_size(axis))]
    return lax.ppermute(value, axis, pairs)


def gelu_pair(pre_act):
    tangent = jnp.tanh(gelu_coef * (pre_act + cubic_coef * pre_act * pre_act * pre_act))
    activated = 0.5 * pre_act * (1.0 + tangent)
    derivative = 0.5 * (1.0 + tangent) + 0.5 * pre_act * (1.0 - tangent * tangent) * gelu_coef * (
        1.0 + 3.0 * cubic_coef * pre_act * pre_act
    )
    return (activated, derivative)


def per_device(
    inputs, out_grad, home_block, blocks_up, blocks_down, up_left, up_right, down_left, down_right
):
    single = jnp.float32
    half_type = jnp.bfloat16
    highest = lax.Precision.HIGHEST
    row_count, width_dev = inputs.shape
    hid_blocks, slot_count, shard_rows, blk_size = blocks_up.shape
    level_count = slot_count - 1
    in_blocks = width_dev // blk_size
    hidden_dev = hid_blocks * blk_size
    top_bit = lax.axis_size("hid").bit_length() - 1
    grad_scale = float(lax.axis_size("dp") * row_count) ** (-0.5)
    select = (home_block[:, None] == jnp.arange(in_blocks, dtype=jnp.int32)[None, :]).astype(single)
    full_up, full_down, left_in, right_in, left_out, right_out = (
        lax.all_gather(blocks_up, "dp", axis=2, tiled=True),
        lax.all_gather(blocks_down, "dp", axis=2, tiled=True),
        lax.all_gather(up_left, "dp", axis=1, tiled=True),
        lax.all_gather(up_right, "dp", axis=0, tiled=True),
        lax.all_gather(down_left, "dp", axis=1, tiled=True),
        lax.all_gather(down_right, "dp", axis=0, tiled=True),
    )
    rank_in = lax.psum(jnp.dot(inputs, left_in, preferred_element_type=single), "hid")
    rank_in = rank_in.astype(half_type)
    in_pieces = [inputs]
    grad_pieces = [out_grad]
    for level_idx in range(level_count):
        in_pieces.append(from_partner(inputs, "hid", top_bit - 1 - level_idx))

    def pick_blocks(pieces):
        stacked = jnp.stack(pieces, 0).reshape(slot_count, row_count, in_blocks, blk_size)
        return jnp.take(stacked, home_block, axis=2)

    picked = pick_blocks(in_pieces)
    part_rows = picked
    up_sum = jnp.einsum("sthk,hskn->thn", part_rows, full_up, preferred_element_type=single)
    pre_act = up_sum.reshape(row_count, hidden_dev) + jnp.dot(
        rank_in, right_in, preferred_element_type=single
    )
    activated, derivative = gelu_pair(pre_act)
    hidden = activated.astype(half_type)
    hidden_blocks = hidden.reshape(row_count, hid_blocks, blk_size)
    rank_mid = lax.psum(jnp.dot(hidden, left_out, preferred_element_type=single), "hid").astype(
        half_type
    )
    part_rows = hidden_blocks
    down_sum = jnp.einsum("thk,hskn->sthn", part_rows, full_down, preferred_element_type=single)
    placed = jnp.einsum("sthn,hi->stin", down_sum, select, precision=highest)
    total = placed[0]
    for level_idx in range(level_count):
        arrived = from_partner(placed[level_idx + 1], "hid", top_bit - 1 - level_idx)
        total = total + arrived
    outputs = (
        total.reshape(row_count, width_dev)
        + jnp.dot(rank_mid, right_out, preferred_element_type=single)
    ).astype(half_type)
    rank_back = lax.psum(jnp.dot(out_grad, right_out.T, preferred_element_type=single), "hid")
    rank_back = rank_back.astype(half_type)
    for level_idx in range(level_count):
        grad_pieces.append(from_partner(out_grad, "hid", top_bit - 1 - level_idx))
    grad_picked = pick_blocks(grad_pieces)
    grad_hidden = jnp.einsum(
        "sthn,hskn->thk", grad_picked, full_down, preferred_element_type=single
    )
    grad_pre = (
        (
            grad_hidden.reshape(row_count, hidden_dev)
            + jnp.dot(rank_back, left_out.T, preferred_element_type=single)
        )
        * derivative
    ).astype(half_type)
    rank_grad = lax.psum(
        jnp.dot(grad_pre, right_in.T, preferred_element_type=single), "hid"
    ).astype(half_type)
    grad_blocks = grad_pre.reshape(row_count, hid_blocks, blk_size)
    back_sum = jnp.einsum("thn,hskn->sthk", grad_blocks, full_up, preferred_element_type=single)
    back_placed = jnp.einsum("sthk,hi->stik", back_sum, select, precision=highest)
    back_total = back_placed[0]
    for level_idx in range(level_count):
        arrived = from_partner(back_placed[level_idx + 1], "hid", top_bit - 1 - level_idx)
        back_total = back_total + arrived
    input_grad = (
        back_total.reshape(row_count, width_dev)
        + jnp.dot(rank_grad, left_in.T, preferred_element_type=single)
    ).astype(half_type)
    summed = (
        lax.psum_scatter(
            (
                grad_scale
                * jnp.einsum("sthk,thn->hskn", picked, grad_blocks, preferred_element_type=single)
            ).astype(jnp.bfloat16),
            "dp",
            scatter_dimension=2,
            tiled=True,
        ).astype(jnp.float32),
        lax.psum_scatter(
            (
                grad_scale
                * jnp.einsum(
                    "thk,sthn->hskn", hidden_blocks, grad_picked, preferred_element_type=single
                )
            ).astype(jnp.bfloat16),
            "dp",
            scatter_dimension=2,
            tiled=True,
        ).astype(jnp.float32),
        lax.psum_scatter(
            (grad_scale * jnp.dot(inputs.T, rank_grad, preferred_element_type=single)).astype(
                jnp.bfloat16
            ),
            "dp",
            scatter_dimension=1,
            tiled=True,
        ).astype(jnp.float32),
        lax.psum_scatter(
            (grad_scale * jnp.dot(rank_in.T, grad_pre, preferred_element_type=single)).astype(
                jnp.bfloat16
            ),
            "dp",
            scatter_dimension=0,
            tiled=True,
        ).astype(jnp.float32),
        lax.psum_scatter(
            (grad_scale * jnp.dot(hidden.T, rank_back, preferred_element_type=single)).astype(
                jnp.bfloat16
            ),
            "dp",
            scatter_dimension=1,
            tiled=True,
        ).astype(jnp.float32),
        lax.psum_scatter(
            (grad_scale * jnp.dot(rank_mid.T, out_grad, preferred_element_type=single)).astype(
                jnp.bfloat16
            ),
            "dp",
            scatter_dimension=0,
            tiled=True,
        ).astype(jnp.float32),
    )
    return (outputs, input_grad) + tuple((summed_part.astype(half_type) for summed_part in summed))


def solution(mesh):
    placed = (
        P("dp", "hid"),
        P("dp", "hid"),
        P("hid"),
        P("hid", None, "dp", None),
        P("hid", None, "dp", None),
        P("hid", "dp"),
        P("dp", "hid"),
        P("hid", "dp"),
        P("dp", "hid"),
    )
    return jax.shard_map(
        per_device,
        mesh=mesh,
        in_specs=placed,
        out_specs=(
            P("dp", "hid"),
            P("dp", "hid"),
            P("hid", None, "dp", None),
            P("hid", None, "dp", None),
            P("hid", "dp"),
            P("dp", "hid"),
            P("hid", "dp"),
            P("dp", "hid"),
        ),
        check_vma=False,
    )
```

profile of v0, /device:TPU:8, one launch (start us, length us, event | category | flops | bytes accessed | tf_op | source)
XLA Modules:
  0.0 738.6 jit_solution(1994460682840392459)
XLA Ops:
  9.8 6.8 collective-permute-start
  16.7 2.7 collective-permute-start.1
  20.5 4.7 collective-permute-start.4
  25.2 2.2 collective-permute-start.5
  27.6 49.3 %all-gather = bf16[32,4,512]{2,1,0:T(4,128)(2,1)S(1)} all-gather(bf16[1,4,512]{2,1,0:T(4,128)(2,1)S(1)} %bitcast.138), channel_id=1, replica_groups=mesh['dp'=32,'hid'=16] {'dp'}, dimensions={0}, use_global_device_ids=true | all-gather | bytes 135168 | tf_op jit(solution)/shard_map/all_gather | solution.py:42
  77.2 42.4 %all-gather.3 = bf16[32,4,512]{2,1,0:T(4,128)(2,1)S(1)} all-gather(bf16[1,4,512]{2,1,0:T(4,128)(2,1)S(1)} %bitcast.139), channel_id=1, replica_groups=mesh['dp'=32,'hid'=16] {'dp'}, dimensions={0}, use_global_device_ids=true | all-gather | bytes 135168 | tf_op jit(solution)/shard_map/all_gather | solution.py:45
  119.9 46.7 %all-gather.1 = bf16[32,4,1024]{2,1,0:T(4,128)(2,1)S(1)} all-gather(bf16[1,4,1024]{2,1,0:T(4,128)(2,1)S(1)} %bitcast.136), channel_id=1, replica_groups=mesh['dp'=32,'hid'=16] {'dp'}, dimensions={0}, use_global_device_ids=true | all-gather | bytes 270336 | tf_op jit(solution)/shard_map/all_gather | solution.py:43
  167.6 45.5 %all-reduce.13 = (bf16[256,128]{1,0:T(8,128)(2,1)S(1)}, bf16[256,128]{1,0:T(8,128)(2,1)S(1)}) all-reduce(f32[256,128]{1,0:T(8,128)S(1)} %fusion.57, f32[256,128]{1,0:T(8,128)S(1)} %fusion.59), channel_id=1, replica_groups=mesh['dp'=32,'hid'=16] {'hid'}, use_global_device_ids=true, to_apply=%region_0.2 | all-reduce | flops 65536 | bytes 393216 | tf_op jit(solution)/shard_map/psum | solution.py:47
  213.1 48.1 %all-gather.2 = bf16[32,4,1024]{2,1,0:T(4,128)(2,1)S(1)} all-gather(bf16[1,4,1024]{2,1,0:T(4,128)(2,1)S(1)} %bitcast.137), channel_id=1, replica_groups=mesh['dp'=32,'hid'=16] {'dp'}, dimensions={0}, use_global_device_ids=true | all-gather | bytes 270336 | tf_op jit(solution)/shard_map/all_gather | solution.py:44
  264.7 1.8 pad_maximum_fusion.1
  266.5 1.9 gather_fusion.1
  268.4 3.2 fusion.8
  271.6 2.6 copy.60
  274.2 3.1 fusion.5
  277.4 2.7 copy.89
  285.1 48.0 %all-reduce.14 = (bf16[256,128]{1,0:T(8,128)(2,1)S(1)}, bf16[256,128]{1,0:T(8,128)(2,1)S(1)}) all-reduce(f32[256,128]{1,0:T(8,128)S(1)} %fusion.58, f32[256,128]{1,0:T(8,128)S(1)} %fusion.60), channel_id=1, replica_groups=mesh['dp'=32,'hid'=16] {'hid'}, use_global_device_ids=true, to_apply=%region_1.0 | all-reduce | flops 65536 | bytes 393216 | tf_op jit(solution)/shard_map/psum | solution.py:67
  334.8 2.3 fusion.10
  337.1 2.4 copy.76
  339.7 1.4 dynamic-slice
  343.7 1.4 copy.117
  345.0 2.9 reshape.97
  347.9 1.4 copy-done.3
  349.9 4.1 fusion.16
  354.4 7.7 %collective-permute-start.6 = (f32[256,2,256]{2,1,0:T(2,128)S(1)}, f32[256,2,256]{2,1,0:T(2,128)S(1)}, u32[]{:S(2)}, u32[]{:S(2)}) collective-permute-start(f32[256,2,256]{2,1,0:T(2,128)S(1)} %get-tuple-element.50), channel_id=1, source_target_pairs={{0,8},{1,9},{2,10},{3,11},{4,12},{5,13},{6,14},{7,15},{8,0},{9,1},... | collective-permute-start | bytes 1572872 | tf_op jit(solution)/shard_map/ppermute | solution.py:13
  362.1 1.9 collective-permute-start.7
  364.6 4.1 fusion.13
  369.1 7.0 collective-permute-start.2
  376.1 1.9 collective-permute-start.3
  378.4 62.6 %collective-permute-done.7 = f32[256,2,256]{2,1,0:T(2,128)S(1)} collective-permute-done((f32[256,2,256]{2,1,0:T(2,128)S(1)}, f32[256,2,256]{2,1,0:T(2,128)S(1)}, u32[]{:S(2)}, u32[]{:S(2)}) %collective-permute-start.7) | collective-permute-done | bytes 524320 | tf_op jit(solution)/shard_map/ppermute | solution.py:13
  441.4 10.7 %collective-permute-done.3 = f32[256,2,256]{2,1,0:T(2,128)S(1)} collective-permute-done((f32[256,2,256]{2,1,0:T(2,128)S(1)}, f32[256,2,256]{2,1,0:T(2,128)S(1)}, u32[]{:S(2)}, u32[]{:S(2)}) %collective-permute-start.3) | collective-permute-done | bytes 524320 | tf_op jit(solution)/shard_map/ppermute | solution.py:13
  453.5 52.5 %all-reduce.12.cloned.1.call-done = (bf16[4,3,256,256]{3,0,1,2:T(4,128)(2,1)}, bf16[512,128]{0,1:T(8,128)(2,1)}, bf16[128,1024]{1,0:T(8,128)(2,1)}, bf16[1024,128]{0,1:T(8,128)(2,1)}, bf16[128,512]{1,0:T(8,128)(2,1)}) async-done(((bf16[4,3,256,256]{3,0,1,2:T(4,128)(2,1)}, bf16[512,128]{0,1:T(8,128)(2,1)}, bf16[128,1024]{1,0:T(8,128)(2,1)}, bf16[1024,128]{0,1:T(8,128)(2,1)}, bf16[128,512]{1,0:T(8,128)(2,1)}), ...) | async-done | bytes 2359312
  512.6 218.0 %reduce-scatter.4.cloned.1.call-done = bf16[8,3072]{1,0:T(8,128)(2,1)} async-done(((bf16[256,3072]{1,0:T(8,128)(2,1)}), bf16[8,3072]{1,0:T(8,128)(2,1)}) %reduce-scatter.4.cloned.1.call-update) | async-done | bytes 49168
  (94 shorter events, 29.2 us)
Async XLA Ops:
  7.2 69.8 %copy-start.2 = (bf16[256,512]{1,0:T(8,128)(2,1)S(1)}, bf16[256,512]{1,0:T(8,128)(2,1)}, u32[]{:S(2)}) copy-start(bf16[256,512]{1,0:T(8,128)(2,1)} %param.11) | copy-start | bytes 786436
  7.2 112.5 %copy-start.1 = (bf16[256,512]{1,0:T(8,128)(2,1)S(1)}, bf16[256,512]{1,0:T(8,128)(2,1)}, u32[]{:S(2)}) copy-start(bf16[256,512]{1,0:T(8,128)(2,1)} %param.12) | copy-start | bytes 786436
  7.2 20.4 %copy-start.12 = (bf16[512,4]{0,1:T(4,128)(2,1)S(1)}, bf16[512,4]{0,1:T(4,128)(2,1)}, u32[]{:S(2)}) copy-start(bf16[512,4]{0,1:T(4,128)(2,1)} %param.16) | copy-start | bytes 12292
  7.2 70.0 %copy-start.13 = (bf16[4,512]{1,0:T(4,128)(2,1)S(1)}, bf16[4,512]{1,0:T(4,128)(2,1)}, u32[]{:S(2)}) copy-start(bf16[4,512]{1,0:T(4,128)(2,1)} %param.19) | copy-start | bytes 12292
  7.2 261.2 %all-gather.7.cloned.1.call-start = ((), (), s32[]{:S(2)}) async-start(), calls=%async_computation.1 | async-start | bytes 1622016 | tf_op jit(solution)/shard_map/all_gather | solution.py:40
  7.9 266.3 %all-gather.9.cloned.1.call-start = ((), (), s32[]{:S(2)}) async-start(), calls=%async_computation.2 | async-start | bytes 1622016 | tf_op jit(solution)/shard_map/all_gather | solution.py:41
  8.7 497.2 %all-reduce.12.cloned.1.call-start = ((), (), s32[]{:S(2)}) async-start(), calls=%async_computation.4 | async-start | bytes 4718592
  9.8 110.1 %copy-start.10 = (bf16[4,1024]{1,0:T(4,128)(2,1)S(1)}, bf16[4,1024]{1,0:T(4,128)(2,1)}, u32[]{:S(2)}) copy-start(bf16[4,1024]{1,0:T(4,128)(2,1)} %param.17) | copy-start | bytes 24580
  9.8 252.2 %collective-permute-start = (bf16[256,512]{0,1:T(8,128)(2,1)S(1)}, bf16[256,512]{0,1:T(8,128)(2,1)S(1)}, u32[]{:S(2)}, u32[]{:S(2)}) collective-permute-start(bf16[256,512]{0,1:T(8,128)(2,1)S(1)} %copy.54), channel_id=1, source_target_pairs={{0,8},{1,9},{2,10},{3,11},{4,12},{5,13},{6,14},{7,15},{8,0},{9,1},... | collective-permute-start | bytes 786440 | tf_op jit(solution)/shard_map/ppermute | solution.py:13
  16.7 245.5 %collective-permute-start.1 = (bf16[256,512]{0,1:T(8,128)(2,1)S(1)}, bf16[256,512]{0,1:T(8,128)(2,1)S(1)}, u32[]{:S(2)}, u32[]{:S(2)}) collective-permute-start(bf16[256,512]{0,1:T(8,128)(2,1)S(1)} %copy.54), channel_id=1, source_target_pairs={{0,4},{1,5},{2,6},{3,7},{4,0},{5,1},{6,2},{7,3},{8,12},{9,13},{10,... | collective-permute-start | bytes 786440 | tf_op jit(solution)/shard_map/ppermute | solution.py:13
  20.5 241.8 %collective-permute-start.4 = (bf16[256,512]{0,1:T(8,128)(2,1)S(1)}, bf16[256,512]{0,1:T(8,128)(2,1)S(1)}, u32[]{:S(2)}, u32[]{:S(2)}) collective-permute-start(bf16[256,512]{0,1:T(8,128)(2,1)S(1)} %copy.63), channel_id=1, source_target_pairs={{0,8},{1,9},{2,10},{3,11},{4,12},{5,13},{6,14},{7,15},{8,0},{9,1},... | collective-permute-start | bytes 786440 | tf_op jit(solution)/shard_map/ppermute | solution.py:13
  25.2 237.9 %collective-permute-start.5 = (bf16[256,512]{0,1:T(8,128)(2,1)S(1)}, bf16[256,512]{0,1:T(8,128)(2,1)S(1)}, u32[]{:S(2)}, u32[]{:S(2)}) collective-permute-start(bf16[256,512]{0,1:T(8,128)(2,1)S(1)} %copy.63), channel_id=1, source_target_pairs={{0,4},{1,5},{2,6},{3,7},{4,0},{5,1},{6,2},{7,3},{8,12},{9,13},{10,... | collective-permute-start | bytes 786440 | tf_op jit(solution)/shard_map/ppermute | solution.py:13
  27.6 139.9 %copy-start.14 = (s32[4]{0:T(128)S(1)}, s32[4]{0:T(128)}, u32[]{:S(2)}) copy-start(s32[4]{0:T(128)} %param.13) | copy-start | bytes 52
  77.0 136.1 %copy-start.11 = (bf16[1024,4]{0,1:T(4,128)(2,1)S(1)}, bf16[1024,4]{0,1:T(4,128)(2,1)}, u32[]{:S(2)}) copy-start(bf16[1024,4]{0,1:T(4,128)(2,1)} %param.18) | copy-start | bytes 24580
  264.7 3.6 copy-start.4
  271.6 2.7 copy-start.6
  277.4 2.7 copy-start.8
  280.1 0.9 copy-start.7
  280.1 1.3 copy-start.9
  339.5 3.3 copy-start.5
  339.5 391.1 %reduce-scatter.4.cloned.1.call-start = ((), (), s32[]{:S(2)}) async-start(), calls=%async_computation.3 | async-start | bytes 1622016
  347.9 1.4 copy-start.3
  354.0 10.0 %copy-start = (bf16[4,3,256,256]{3,2,1,0:T(8,128)(2,1)S(1)}, bf16[4,3,256,256]{3,2,1,0:T(8,128)(2,1)}, u32[]{:S(2)}) copy-start(bf16[4,3,256,256]{3,2,1,0:T(8,128)(2,1)} %all-gather.9.cloned.1.call-done) | copy-start | bytes 4718596
  354.4 24.0 %collective-permute-start.6 = (f32[256,2,256]{2,1,0:T(2,128)S(1)}, f32[256,2,256]{2,1,0:T(2,128)S(1)}, u32[]{:S(2)}, u32[]{:S(2)}) collective-permute-start(f32[256,2,256]{2,1,0:T(2,128)S(1)} %get-tuple-element.50), channel_id=1, source_target_pairs={{0,8},{1,9},{2,10},{3,11},{4,12},{5,13},{6,14},{7,15},{8,0},{9,1},... | collective-permute-start | bytes 1572872 | tf_op jit(solution)/shard_map/ppermute | solution.py:13
  362.1 78.9 %collective-permute-start.7 = (f32[256,2,256]{2,1,0:T(2,128)S(1)}, f32[256,2,256]{2,1,0:T(2,128)S(1)}, u32[]{:S(2)}, u32[]{:S(2)}) collective-permute-start(f32[256,2,256]{2,1,0:T(2,128)S(1)} %get-tuple-element.51), channel_id=1, source_target_pairs={{0,4},{1,5},{2,6},{3,7},{4,0},{5,1},{6,2},{7,3},{8,12},{9,13},{10,... | collective-permute-start | bytes 1572872 | tf_op jit(solution)/shard_map/ppermute | solution.py:13
  369.1 72.3 %collective-permute-start.2 = (f32[256,2,256]{2,1,0:T(2,128)S(1)}, f32[256,2,256]{2,1,0:T(2,128)S(1)}, u32[]{:S(2)}, u32[]{:S(2)}) collective-permute-start(f32[256,2,256]{2,1,0:T(2,128)S(1)} %get-tuple-element.52), channel_id=1, source_target_pairs={{0,8},{1,9},{2,10},{3,11},{4,12},{5,13},{6,14},{7,15},{8,0},{9,1},... | collective-permute-start | bytes 1572872 | tf_op jit(solution)/shard_map/ppermute | solution.py:13
  376.1 76.1 %collective-permute-start.3 = (f32[256,2,256]{2,1,0:T(2,128)S(1)}, f32[256,2,256]{2,1,0:T(2,128)S(1)}, u32[]{:S(2)}, u32[]{:S(2)}) collective-permute-start(f32[256,2,256]{2,1,0:T(2,128)S(1)} %get-tuple-element.53), channel_id=1, source_target_pairs={{0,4},{1,5},{2,6},{3,7},{4,0},{5,1},{6,2},{7,3},{8,12},{9,13},{10,... | collective-permute-start | bytes 1572872 | tf_op jit(solution)/shard_map/ppermute | solution.py:13
Sparse Core Ops, SparseCore 0:
  11.1 83.7 all-gather.6
  97.9 77.6 all-gather.8
  339.6 166.2 all-reduce.11
  510.8 219.7 reduce-scatter.3
where the time goes:
time: 740 us; the launch traced here: 739 us
  waiting for transfers between devices  345 us (47%)
  blocking collectives  280 us (38%)
  starting transfers between devices  35.3 us (5%)
  local copies, waits for them, and re-layouts  33.8 us (5%)
  matrix products  25.2 us (3%)
  between operations  15.6 us (2%)
    unnamed x6, waiting for transfers between devices  272 us
    ppermute x8, waiting for transfers between devices, from_partner(): return lax.ppermute(value, axis, pairs)  73.3 us
    all_gather x1, blocking collectives, per_device(): lax.all_gather(up_left, 'dp', axis=1, tiled=True)  49.3 us
    all_gather x1, blocking collectives, per_device(): lax.all_gather(down_left, 'dp', axis=1, tiled=True)  48.1 us
    psum x1, blocking collectives, per_device(): lax.psum(jnp.dot(hidden, left_out, preferred_element_type=single), 'hid')  48 us
    all_gather x1, blocking collectives, per_device(): lax.all_gather(up_right, 'dp', axis=0, tiled=True)  46.7 us
    psum x1, blocking collectives, per_device(): lax.psum(jnp.dot(inputs, left_in, preferred_element_type=single), 'hid')  45.5 us
    all_gather x1, blocking collectives, per_device(): lax.all_gather(down_right, 'dp', axis=0, tiled=True)  42.4 us
  transfers between devices with their start and end apart: 12, of which 4 were waited for; matrix products, arithmetic and copies ran while one was open for 6% of the time, Pallas kernels for 0%

commit v1 on v0

--- a/solution.py
+++ b/solution.py
@@ -5,6 +5,18 @@
 
 gelu_coef = 0.7978845608028654
 cubic_coef = 0.044715
+
+
+def doubled_up(x, axis, dim):
+    ways, here = (lax.axis_size(axis), lax.axis_index(axis))
+    grown, reach = (x, 1)
+    while reach < ways:
+        theirs = lax.ppermute(grown, axis, [(d, d ^ reach) for d in range(ways)])
+        mine_first = jnp.concatenate([grown, theirs], axis=dim)
+        theirs_first = jnp.concatenate([theirs, grown], axis=dim)
+        grown = jnp.where(here & reach == 0, mine_first, theirs_first)
+        reach = 2 * reach
+    return grown
 
 
 def from_partner(value, axis, distance):
@@ -40,7 +52,7 @@
         lax.all_gather(blocks_up, "dp", axis=2, tiled=True),
         lax.all_gather(blocks_down, "dp", axis=2, tiled=True),
         lax.all_gather(up_left, "dp", axis=1, tiled=True),
-        lax.all_gather(up_right, "dp", axis=0, tiled=True),
+        doubled_up(up_right, "dp", 0),
         lax.all_gather(down_left, "dp", axis=1, tiled=True),
         lax.all_gather(down_right, "dp", axis=0, tiled=True),
     )

time: 740 us -> 716 us (0.968)
  blocking collectives: 280 us -> 233 us
  starting transfers between devices: 35.3 us -> 53.1 us
    all_gather x1 -> x0, blocking collectives: 46.7 us -> none  [per_device(): lax.all_gather(up_right, 'dp', axis=0, tiled=True)]
    ppermute x0 -> x5, starting transfers between devices: none -> 18 us  [doubled_up(): theirs = lax.ppermute(grown, axis, [(d, d ^ reach) for d in range(ways)])]
    unnamed x49 -> x42, local copies, waits for them, and re-layouts: 19.2 us -> 17.8 us
  transfers between devices with their start and end apart: 12 -> 17, of which waited for: 4 -> 5; matrix products, arithmetic and copies ran while one was open for 6% -> 7% of each run, Pallas kernels for 0% -> 0%
where the time goes in v1:
time: 716 us; the launch traced here: 715 us
  waiting for transfers between devices  349 us (49%)
  blocking collectives  233 us (33%)
  starting transfers between devices  53.1 us (7%)
  local copies, waits for them, and re-layouts  31.1 us (4%)
  matrix products  29.9 us (4%)
  between operations  15.6 us (2%)
    unnamed x6, waiting for transfers between devices  273 us
    ppermute x8, waiting for transfers between devices, from_partner(): return lax.ppermute(value, axis, pairs)  73.1 us
    all_gather x1, blocking collectives, per_device(): lax.all_gather(down_left, 'dp', axis=1, tiled=True)  48.4 us
    all_gather x1, blocking collectives, per_device(): lax.all_gather(up_left, 'dp', axis=1, tiled=True)  48.2 us
    psum x1, blocking collectives, per_device(): lax.psum(jnp.dot(hidden, left_out, preferred_element_type=single), 'hid')  48 us
    psum x1, blocking collectives, per_device(): lax.psum(jnp.dot(inputs, left_in, preferred_element_type=single), 'hid')  46.7 us
    all_gather x1, blocking collectives, per_device(): lax.all_gather(down_right, 'dp', axis=0, tiled=True)  41.7 us
    ppermute x8, starting transfers between devices, from_partner(): return lax.ppermute(value, axis, pairs)  34.8 us
  transfers between devices with their start and end apart: 17, of which 5 were waited for; matrix products, arithmetic and copies ran while one was open for 7% of the time, Pallas kernels for 0%

profile of v1, /device:TPU:8, one launch (start us, length us, event | category | flops | bytes accessed | tf_op | source)
XLA Modules:
  0.0 715.1 jit_solution(6504140945987221768)
XLA Ops:
  9.8 6.8 collective-permute-start
  16.7 2.7 collective-permute-start.1
  20.5 4.7 collective-permute-start.9
  25.2 2.2 collective-permute-start.10
  27.4 4.3 collective-permute-start.2
  31.7 48.2 %all-gather = bf16[32,4,512]{2,1,0:T(4,128)(2,1)S(1)} all-gather(bf16[1,4,512]{2,1,0:T(4,128)(2,1)} %bitcast.134), channel_id=1, replica_groups=mesh['dp'=32,'hid'=16] {'dp'}, dimensions={0}, use_global_device_ids=true | all-gather | bytes 135168 | tf_op jit(solution)/shard_map/all_gather | solution.py:54
  80.0 41.7 %all-gather.2 = bf16[32,4,512]{2,1,0:T(4,128)(2,1)S(1)} all-gather(bf16[1,4,512]{2,1,0:T(4,128)(2,1)} %bitcast.135), channel_id=1, replica_groups=mesh['dp'=32,'hid'=16] {'dp'}, dimensions={0}, use_global_device_ids=true | all-gather | bytes 135168 | tf_op jit(solution)/shard_map/all_gather | solution.py:57
  122.3 2.2 collective-permute-start.3
  124.4 46.7 %all-reduce.13 = (bf16[256,128]{1,0:T(8,128)(2,1)}, bf16[256,128]{1,0:T(8,128)(2,1)}) all-reduce(f32[256,128]{1,0:T(8,128)S(1)} %fusion.60, f32[256,128]{1,0:T(8,128)S(1)} %fusion.62), channel_id=1, replica_groups=mesh['dp'=32,'hid'=16] {'hid'}, use_global_device_ids=true, to_apply=%region_0.2 | all-reduce | flops 65536 | bytes 393216 | tf_op jit(solution)/shard_map/psum | solution.py:59
  172.1 5.0 collective-permute-start.4
  177.1 48.4 %all-gather.1 = bf16[32,4,1024]{2,1,0:T(4,128)(2,1)S(1)} all-gather(bf16[1,4,1024]{2,1,0:T(4,128)(2,1)S(1)} %bitcast.133), channel_id=1, replica_groups=mesh['dp'=32,'hid'=16] {'dp'}, dimensions={0}, use_global_device_ids=true | all-gather | bytes 270336 | tf_op jit(solution)/shard_map/all_gather | solution.py:56
  225.6 3.0 collective-permute-start.5
  228.5 3.2 collective-permute-done.5
  231.7 3.6 collective-permute-start.6
  241.8 3.1 fusion.8
  244.9 3.7 fusion.5
  250.1 2.5 copy.89
  252.6 2.6 multiply_convert_fusion.2
  257.0 2.0 fusion.20
  261.3 48.0 %all-reduce.14 = (bf16[256,128]{1,0:T(8,128)(2,1)S(1)}, bf16[256,128]{1,0:T(8,128)(2,1)S(1)}) all-reduce(f32[256,128]{1,0:T(8,128)S(1)} %fusion.61, f32[256,128]{1,0:T(8,128)S(1)} %fusion.39), channel_id=1, replica_groups=mesh['dp'=32,'hid'=16] {'hid'}, use_global_device_ids=true, to_apply=%region_1.3 | all-reduce | flops 65536 | bytes 393216 | tf_op jit(solution)/shard_map/psum | solution.py:79
  311.0 2.3 fusion.10
  313.3 2.3 copy.76
  321.2 2.9 reshape.95
  326.1 4.1 fusion.13
  330.5 7.5 %collective-permute-start.7 = (f32[256,2,256]{2,1,0:T(2,128)S(1)}, f32[256,2,256]{2,1,0:T(2,128)S(1)}, u32[]{:S(2)}, u32[]{:S(2)}) collective-permute-start(f32[256,2,256]{2,1,0:T(2,128)S(1)} %get-tuple-element.52), channel_id=1, source_target_pairs={{0,8},{1,9},{2,10},{3,11},{4,12},{5,13},{6,14},{7,15},{8,0},{9,1},... | collective-permute-start | bytes 1572872 | tf_op jit(solution)/shard_map/ppermute | solution.py:25
  338.0 1.9 collective-permute-start.8
  340.6 4.1 fusion.16
  345.0 7.0 collective-permute-start.11
  354.4 62.4 %collective-permute-done.8 = f32[256,2,256]{2,1,0:T(2,128)S(1)} collective-permute-done((f32[256,2,256]{2,1,0:T(2,128)S(1)}, f32[256,2,256]{2,1,0:T(2,128)S(1)}, u32[]{:S(2)}, u32[]{:S(2)}) %collective-permute-start.8) | collective-permute-done | bytes 524320 | tf_op jit(solution)/shard_map/ppermute | solution.py:25
  417.2 10.7 %collective-permute-done.12 = f32[256,2,256]{2,1,0:T(2,128)S(1)} collective-permute-done((f32[256,2,256]{2,1,0:T(2,128)S(1)}, f32[256,2,256]{2,1,0:T(2,128)S(1)}, u32[]{:S(2)}, u32[]{:S(2)}) %collective-permute-start.12) | collective-permute-done | bytes 524320 | tf_op jit(solution)/shard_map/ppermute | solution.py:25
  429.3 53.1 %all-reduce.12.cloned.1.call-done = (bf16[4,3,256,256]{3,0,1,2:T(4,128)(2,1)}, bf16[512,128]{0,1:T(8,128)(2,1)}, bf16[128,1024]{1,0:T(8,128)(2,1)}, bf16[1024,128]{0,1:T(8,128)(2,1)}, bf16[128,512]{1,0:T(8,128)(2,1)}) async-done(((bf16[4,3,256,256]{3,0,1,2:T(4,128)(2,1)}, bf16[512,128]{0,1:T(8,128)(2,1)}, bf16[128,1024]{1,0:T(8,128)(2,1)}, bf16[1024,128]{0,1:T(8,128)(2,1)}, bf16[128,512]{1,0:T(8,128)(2,1)}), ...) | async-done | bytes 2359312
  489.1 218.0 %reduce-scatter.4.cloned.1.call-done = bf16[8,3072]{1,0:T(8,128)(2,1)} async-done(((bf16[256,3072]{1,0:T(8,128)(2,1)}), bf16[8,3072]{1,0:T(8,128)(2,1)}) %reduce-scatter.4.cloned.1.call-update) | async-done | bytes 49168
  (100 shorter events, 38.8 us)
Async XLA Ops:
  7.2 114.6 %copy-start.2 = (bf16[256,512]{1,0:T(8,128)(2,1)S(1)}, bf16[256,512]{1,0:T(8,128)(2,1)}, u32[]{:S(2)}) copy-start(bf16[256,512]{1,0:T(8,128)(2,1)} %param.11) | copy-start | bytes 786436
  7.2 114.8 %copy-start.1 = (bf16[256,512]{1,0:T(8,128)(2,1)S(1)}, bf16[256,512]{1,0:T(8,128)(2,1)}, u32[]{:S(2)}) copy-start(bf16[256,512]{1,0:T(8,128)(2,1)} %param.12) | copy-start | bytes 786436
  7.2 115.0 %copy-start.9 = (bf16[4,1024]{1,0:T(4,128)(2,1)S(1)}, bf16[4,1024]{1,0:T(4,128)(2,1)}, u32[]{:S(2)}) copy-start(bf16[4,1024]{1,0:T(4,128)(2,1)} %param.17) | copy-start | bytes 24580
  7.2 114.5 %copy-start.10 = (s32[4]{0:T(128)S(1)}, s32[4]{0:T(128)}, u32[]{:S(2)}) copy-start(s32[4]{0:T(128)} %param.13) | copy-start | bytes 52
  7.2 234.5 %all-gather.6.cloned.1.call-start = ((), (), s32[]{:S(2)}) async-start(), calls=%async_computation.1 | async-start | bytes 1622016 | tf_op jit(solution)/shard_map/all_gather | solution.py:52
  7.9 236.9 %all-gather.8.cloned.1.call-start = ((), (), s32[]{:S(2)}) async-start(), calls=%async_computation.2 | async-start | bytes 1622016 | tf_op jit(solution)/shard_map/all_gather | solution.py:53
  8.7 473.7 %all-reduce.12.cloned.1.call-start = ((), (), s32[]{:S(2)}) async-start(), calls=%async_computation.4 | async-start | bytes 4718592
  9.8 225.5 %collective-permute-start = (bf16[256,512]{0,1:T(8,128)(2,1)S(1)}, bf16[256,512]{0,1:T(8,128)(2,1)S(1)}, u32[]{:S(2)}, u32[]{:S(2)}) collective-permute-start(bf16[256,512]{0,1:T(8,128)(2,1)S(1)} %copy.54), channel_id=1, source_target_pairs={{0,8},{1,9},{2,10},{3,11},{4,12},{5,13},{6,14},{7,15},{8,0},{9,1},... | collective-permute-start | bytes 786440 | tf_op jit(solution)/shard_map/ppermute | solution.py:25
  16.7 218.8 %collective-permute-start.1 = (bf16[256,512]{0,1:T(8,128)(2,1)S(1)}, bf16[256,512]{0,1:T(8,128)(2,1)S(1)}, u32[]{:S(2)}, u32[]{:S(2)}) collective-permute-start(bf16[256,512]{0,1:T(8,128)(2,1)S(1)} %copy.54), channel_id=1, source_target_pairs={{0,4},{1,5},{2,6},{3,7},{4,0},{5,1},{6,2},{7,3},{8,12},{9,13},{10,... | collective-permute-start | bytes 786440 | tf_op jit(solution)/shard_map/ppermute | solution.py:25
  20.5 215.2 %collective-permute-start.9 = (bf16[256,512]{0,1:T(8,128)(2,1)S(1)}, bf16[256,512]{0,1:T(8,128)(2,1)S(1)}, u32[]{:S(2)}, u32[]{:S(2)}) collective-permute-start(bf16[256,512]{0,1:T(8,128)(2,1)S(1)} %copy.63), channel_id=1, source_target_pairs={{0,8},{1,9},{2,10},{3,11},{4,12},{5,13},{6,14},{7,15},{8,0},{9,1},... | collective-permute-start | bytes 786440 | tf_op jit(solution)/shard_map/ppermute | solution.py:25
  25.2 211.3 %collective-permute-start.10 = (bf16[256,512]{0,1:T(8,128)(2,1)S(1)}, bf16[256,512]{0,1:T(8,128)(2,1)S(1)}, u32[]{:S(2)}, u32[]{:S(2)}) collective-permute-start(bf16[256,512]{0,1:T(8,128)(2,1)S(1)} %copy.63), channel_id=1, source_target_pairs={{0,4},{1,5},{2,6},{3,7},{4,0},{5,1},{6,2},{7,3},{8,12},{9,13},{10,... | collective-permute-start | bytes 786440 | tf_op jit(solution)/shard_map/ppermute | solution.py:25
  27.4 94.8 %collective-permute-start.2 = (bf16[4,1024]{1,0:T(4,128)(2,1)}, bf16[4,1024]{1,0:T(4,128)(2,1)S(1)}, u32[]{:S(2)}, u32[]{:S(2)}) collective-permute-start(bf16[4,1024]{1,0:T(4,128)(2,1)} %param.17), channel_id=1, source_target_pairs={{0,16},{16,0},{32,48},{48,32},{64,80},{80,64},{96,112},{112,96},{1... | collective-permute-start | bytes 24584 | tf_op jit(solution)/shard_map/ppermute | solution.py:14
  79.9 97.1 %copy-start.8 = (bf16[1024,4]{0,1:T(4,128)(2,1)S(1)}, bf16[1024,4]{0,1:T(4,128)(2,1)}, u32[]{:S(2)}) copy-start(bf16[1024,4]{0,1:T(4,128)(2,1)} %param.18) | copy-start | bytes 24580
  122.3 49.8 %collective-permute-start.3 = (bf16[8,1024]{1,0:T(8,128)(2,1)S(1)}, bf16[8,1024]{1,0:T(8,128)(2,1)S(1)}, u32[]{:S(2)}, u32[]{:S(2)}) collective-permute-start(bf16[8,1024]{1,0:T(8,128)(2,1)S(1)} %maximum_select_fusion.6), channel_id=1, source_target_pairs={{0,32},{16,48},{32,0},{48,16},{64,96},{80,112},{96,64},{112,80},{1... | collective-permute-start | bytes 49160 | tf_op jit(solution)/shard_map/ppermute | solution.py:14
  172.1 53.4 %collective-permute-start.4 = (bf16[16,1024]{1,0:T(8,128)(2,1)S(1)}, bf16[16,1024]{1,0:T(8,128)(2,1)S(1)}, u32[]{:S(2)}, u32[]{:S(2)}) collective-permute-start(bf16[16,1024]{1,0:T(8,128)(2,1)S(1)} %maximum_select_fusion.5), channel_id=1, source_target_pairs={{0,64},{16,80},{32,96},{48,112},{64,0},{80,16},{96,32},{112,48},{1... | collective-permute-start | bytes 98312 | tf_op jit(solution)/shard_map/ppermute | solution.py:14
  225.6 6.2 collective-permute-start.5
  231.7 20.9 %collective-permute-start.6 = (bf16[64,1024]{1,0:T(8,128)(2,1)S(1)}, bf16[64,1024]{1,0:T(8,128)(2,1)}, u32[]{:S(2)}, u32[]{:S(2)}) collective-permute-start(bf16[64,1024]{1,0:T(8,128)(2,1)S(1)} %maximum_select_fusion.1), channel_id=1, source_target_pairs={{0,256},{16,272},{32,288},{48,304},{64,320},{80,336},{96,352},{112... | collective-permute-start | bytes 393224 | tf_op jit(solution)/shard_map/ppermute | solution.py:14
  238.1 3.6 copy-start.4
  250.1 2.6 copy-start.6
  255.2 0.8 copy-start.7
  255.6 1.5 copy-start.11
  315.6 3.3 copy-start.5
  315.7 391.4 %reduce-scatter.4.cloned.1.call-start = ((), (), s32[]{:S(2)}) async-start(), calls=%async_computation.3 | async-start | bytes 1622016
  324.1 1.4 copy-start
  330.2 9.8 %copy-start.3 = (bf16[4,3,256,256]{3,2,1,0:T(8,128)(2,1)S(1)}, bf16[4,3,256,256]{3,2,1,0:T(8,128)(2,1)}, u32[]{:S(2)}) copy-start(bf16[4,3,256,256]{3,2,1,0:T(8,128)(2,1)} %all-gather.6.cloned.1.call-done) | copy-start | bytes 4718596
  330.5 23.8 %collective-permute-start.7 = (f32[256,2,256]{2,1,0:T(2,128)S(1)}, f32[256,2,256]{2,1,0:T(2,128)S(1)}, u32[]{:S(2)}, u32[]{:S(2)}) collective-permute-start(f32[256,2,256]{2,1,0:T(2,128)S(1)} %get-tuple-element.52), channel_id=1, source_target_pairs={{0,8},{1,9},{2,10},{3,11},{4,12},{5,13},{6,14},{7,15},{8,0},{9,1},... | collective-permute-start | bytes 1572872 | tf_op jit(solution)/shard_map/ppermute | solution.py:25
  338.0 78.8 %collective-permute-start.8 = (f32[256,2,256]{2,1,0:T(2,128)S(1)}, f32[256,2,256]{2,1,0:T(2,128)S(1)}, u32[]{:S(2)}, u32[]{:S(2)}) collective-permute-start(f32[256,2,256]{2,1,0:T(2,128)S(1)} %get-tuple-element.53), channel_id=1, source_target_pairs={{0,4},{1,5},{2,6},{3,7},{4,0},{5,1},{6,2},{7,3},{8,12},{9,13},{10,... | collective-permute-start | bytes 1572872 | tf_op jit(solution)/shard_map/ppermute | solution.py:25
  345.0 72.2 %collective-permute-start.11 = (f32[256,2,256]{2,1,0:T(2,128)S(1)}, f32[256,2,256]{2,1,0:T(2,128)S(1)}, u32[]{:S(2)}, u32[]{:S(2)}) collective-permute-start(f32[256,2,256]{2,1,0:T(2,128)S(1)} %get-tuple-element.50), channel_id=1, source_target_pairs={{0,8},{1,9},{2,10},{3,11},{4,12},{5,13},{6,14},{7,15},{8,0},{9,1},... | collective-permute-start | bytes 1572872 | tf_op jit(solution)/shard_map/ppermute | solution.py:25
  352.0 75.9 %collective-permute-start.12 = (f32[256,2,256]{2,1,0:T(2,128)S(1)}, f32[256,2,256]{2,1,0:T(2,128)S(1)}, u32[]{:S(2)}, u32[]{:S(2)}) collective-permute-start(f32[256,2,256]{2,1,0:T(2,128)S(1)} %get-tuple-element.51), channel_id=1, source_target_pairs={{0,4},{1,5},{2,6},{3,7},{4,0},{5,1},{6,2},{7,3},{8,12},{9,13},{10,... | collective-permute-start | bytes 1572872 | tf_op jit(solution)/shard_map/ppermute | solution.py:25
Sparse Core Ops, SparseCore 0:
  11.1 83.8 all-gather.5
  98.0 77.4 all-gather.7
  315.8 166.6 all-reduce.11
  487.3 219.7 reduce-scatter.3
